TPU v7x, 32 devices: a whole 2x2x4 slice. The times are simulated.
32 devices in a mesh: gx: 4 (over x, core), gy: 8 (over z, y).
Axes of the slice: x: 2, y: 2, z: 4, core: 2. Of those that a mesh axis runs over, the one named last changes fastest.
Arguments:
- features: bfloat16 [4, 8, 2, 96, 4096], P('gx', 'gy'), may hold values from -6 to 6
- grad_out: bfloat16 [4, 8, 2, 96, 4096], P('gx', 'gy'), may hold values from -6 to 6
- weight: bfloat16 [96, 2592], replicated, may hold values from -0.125 to 0.125
- active: int32 [4, 8, 2], P('gx', 'gy'), may hold values from 0 to 1, as said below
Outputs:
- out: bfloat16 [4, 8, 2, 96, 4096], P('gx', 'gy')
- grad_in: bfloat16 [4, 8, 2, 96, 4096], P('gx', 'gy')
- grad_weight: float32 [248832], P(('gx', 'gy'))
Inputs may be any that keep to these rules, and one draw needn't show every extreme that they name: The two columns with the same gx index and gy indices 2m and 2m + 1 hold exactly 2 active bricks together, so a column holds 0 to 2 of them; some column holds 2 in every draw.
All inputs are finite; a program needn't handle non-finite values.
Results may differ from a plain program's by a relative error of at most 0.001.
Values may be sent and summed in bfloat16 or wider, within the bound.
A program may use at most 128 MiB of HBM per device.

v0:
```python
import functools
import math

import jax
import jax.numpy as jnp
from jax import lax
from jax.experimental import pallas as pl
from jax.experimental.pallas import tpu as pltpu
from jax.sharding import PartitionSpec as P

EDGE = 16
PLANE = EDGE * EDGE
MESH = pl.DeviceIdType.MESH
AXES = ("gx", "gy")


def lanes(shape):
    return lax.broadcasted_iota(jnp.int32, shape, 1)


def side_faces(counts):
    here = [lax.axis_index(axis) for axis in AXES]
    faces = []
    for dim, axis in enumerate(AXES):
        for step in (-1, 1):
            exists = here[dim] > 0 if step < 0 else here[dim] < counts[dim] - 1
            faces.append((exists, {axis: here[dim] + step}))
    return faces


def fill_faces(act_ref, ref, send):
    levels, channels, _ = ref.shape
    rows = lanes((channels, PLANE)) // EDGE
    last = (EDGE - 1) * PLANE
    for level in range(levels):
        live = act_ref[0, level].astype(jnp.bfloat16)
        send[0, level] = ref[level, :, :PLANE] * live
        send[1, level] = ref[level, :, last : last + PLANE] * live
        south = jnp.zeros((channels, PLANE), jnp.float32)
        north = jnp.zeros((channels, PLANE), jnp.float32)
        for x in range(EDGE):
            plane = ref[level, :, x * PLANE : (x + 1) * PLANE].astype(jnp.float32)
            south = jnp.where(rows == x, pltpu.roll(plane, x * EDGE, 1), south)
            shift = (x * EDGE + EDGE) % PLANE
            north = jnp.where(rows == x, pltpu.roll(plane, shift, 1), north)
        send[2, level] = south.astype(jnp.bfloat16) * live
        send[3, level] = north.astype(jnp.bfloat16) * live


def face_copy(faces, send, recv, send_sem, recv_sem, side, slot):
    return pltpu.make_async_remote_copy(
        src_ref=send.at[side],
        dst_ref=recv.at[slot],
        send_sem=send_sem.at[side],
        recv_sem=recv_sem.at[slot],
        device_id=faces[side][1],
        device_id_type=MESH,
    )


def send_faces(faces, send, recv, send_sem, recv_sem):
    for side in range(4):

        @pl.when(faces[side][0])
        def _():
            face_copy(faces, send, recv, send_sem, recv_sem, side, side ^ 1).start()

        @pl.when(jnp.logical_not(faces[side][0]))
        def _():
            recv[side] = jnp.zeros(recv.shape[1:], jnp.bfloat16)


def await_faces(faces, send, recv, send_sem, recv_sem):
    for side in range(4):

        @pl.when(faces[side][0])
        def _():
            face_copy(faces, send, recv, send_sem, recv_sem, side, side ^ 1).wait_send()
            face_copy(faces, send, recv, send_sem, recv_sem, side, side).wait_recv()


def lay_cube(act_ref, ref, cube):
    levels, channels, _ = ref.shape
    zero = jnp.zeros((channels, PLANE), jnp.bfloat16)
    for level in range(levels):
        live = act_ref[0, level].astype(jnp.bfloat16)
        cube[level, 0] = zero
        cube[level, EDGE + 1] = zero
        for x in range(EDGE):
            cube[level, x + 1] = ref[level, :, x * PLANE : (x + 1) * PLANE] * live


def build_taps(level, levels, cube, halo, taps, at, slot):
    channels = cube.shape[2]
    lane = lanes((channels, PLANE))
    y_at, z_at = lane // EDGE, lane % EDGE
    at = jnp.asarray(at, jnp.int32)

    def roll(values, shift):
        return pltpu.roll(values, shift, 1)

    inner = ((at >= 1) & (at <= EDGE)).astype(jnp.float32)
    base = (at - 1) * EDGE
    west = (at == 0).astype(jnp.bfloat16)
    east = (at == EDGE + 1).astype(jnp.bfloat16)
    here = cube[level, at] + halo[0, level] * west + halo[1, level] * east
    here = here.astype(jnp.float32)
    south = halo[2, level].astype(jnp.float32) * inner
    north = halo[3, level].astype(jnp.float32) * inner
    south = roll(south, (2 * PLANE - base) % PLANE)
    north = roll(north, (2 * PLANE - EDGE - base) % PLANE)
    nears = [cube[k, at].astype(jnp.float32) if 0 <= k < levels else None
             for k in (level - 1, level + 1)]
    for dy in (-1, 0, 1):
        if dy < 0:
            moved = jnp.where(y_at == 0, south, roll(here, EDGE))
        elif dy > 0:
            moved = jnp.where(y_at == EDGE - 1, north, roll(here, PLANE - EDGE))
        else:
            moved = here
        rims = []
        for near, edge in zip(nears, (1 - EDGE, EDGE - 1)):
            if near is None:
                rims.append(0.0)
                continue
            rim = roll(near, (edge - dy * EDGE) % PLANE)
            if dy < 0:
                rim = jnp.where(y_at == 0, 0.0, rim)
            elif dy > 0:
                rim = jnp.where(y_at == EDGE - 1, 0.0, rim)
            rims.append(rim)
        low = jnp.where(z_at == 0, rims[0], roll(moved, 1))
        high = jnp.where(z_at == EDGE - 1, rims[1], roll(moved, PLANE - 1))
        for dz, value in ((-1, low), (0, moved), (1, high)):
            tap = 3 * (dy + 1) + dz + 1
            taps[slot, pl.ds(tap * channels, channels), :] = value.astype(jnp.bfloat16)


def add_plane(w, live, level, taps, carry, ref, at, slot):
    channels = carry.shape[1]
    at = jnp.asarray(at, jnp.int32)
    target = pl.ds(pl.multiple_of(jnp.maximum(at - 2, 0) * PLANE, PLANE), PLANE)
    y = jnp.dot(w[...], taps[slot], preferred_element_type=jnp.float32)
    before, middle, after = (y[i * channels : (i + 1) * channels] for i in range(3))
    ref[level, :, target] = ((after + carry[0]) * live).astype(jnp.bfloat16)
    carry[0] = middle + carry[1]
    carry[1] = before


def run_pairs(first, end, build, multiply):
    def pair(i, unused):
        at = 2 * i
        build(at + 1, 1)
        multiply(at, 0)
        build(jnp.minimum(at + 2, EDGE + 1), 0)
        multiply(at + 1, 1)
        return unused

    lax.fori_loop(first, end, pair, 0)


def ahead_kernel(
    counts, scale, act_ref, f_ref, g_ref, weight_ref, out_ref, gw_ref, w_back, halo_g,
    w, halo_f, send_f, send_g, cube, own, taps, carry, gw, f_sem, f_recv, g_sem, g_recv,
):
    levels, channels, _ = f_ref.shape
    depth = 9 * channels
    faces = side_faces(counts)
    barrier = pltpu.get_barrier_semaphore()
    for exists, target in faces:

        @pl.when(exists)
        def _():
            pl.semaphore_signal(barrier, inc=1, device_id=target, device_id_type=MESH)

    fill_faces(act_ref, f_ref, send_f)
    pl.semaphore_wait(barrier, sum(exists.astype(jnp.int32) for exists, _target in faces))
    send_faces(faces, send_f, halo_f, f_sem, f_recv)
    fill_faces(act_ref, g_ref, send_g)
    send_faces(faces, send_g, halo_g, g_sem, g_recv)

    wide = weight_ref[...].astype(jnp.float32)
    w[...] = jnp.zeros_like(w)
    w_back[...] = jnp.zeros_like(w_back)
    for dx in range(3):
        rows = slice(dx * channels, (dx + 1) * channels)
        w[rows, :depth] = wide[:, dx * depth : (dx + 1) * depth].astype(jnp.bfloat16)
        blocks = []
        for tap in range(9):
            start = ((2 - dx) * 9 + 8 - tap) * channels
            blocks.append(wide[:, start : start + channels].T)
        w_back[rows, :depth] = jnp.concatenate(blocks, axis=1).astype(jnp.bfloat16)

    lay_cube(act_ref, f_ref, cube)
    taps[...] = jnp.zeros_like(taps)
    gw[...] = jnp.zeros_like(gw)
    zero = jnp.zeros((channels, PLANE), jnp.bfloat16)
    for at in (0, 1, EDGE + 2, EDGE + 3):
        own[at] = zero
    await_faces(faces, send_f, halo_f, f_sem, f_recv)

    for level in range(levels):
        live = act_ref[0, level]
        for x in range(EDGE):
            plane = g_ref[level, :, x * PLANE : (x + 1) * PLANE]
            own[x + 2] = plane * live.astype(jnp.bfloat16)
        carry[...] = jnp.zeros_like(carry)

        def build(at, slot):
            build_taps(level, levels, cube, halo_f, taps, at, slot)

        def multiply(at, slot):
            add_plane(w, live.astype(jnp.float32), level, taps, carry, out_ref, at, slot)
            grads = own[pl.ds(at, 3)].reshape(3 * channels, PLANE)
            gw[...] += lax.dot_general(
                grads,
                taps[slot, :depth, :],
                (((1,), (1,)), ((), ())),
                preferred_element_type=jnp.float32,
            )

        build(0, 0)
        run_pairs(0, EDGE // 2 + 1, build, multiply)

    for dx in range(3):
        gw_ref[dx] = gw[(2 - dx) * channels : (3 - dx) * channels, :] * scale
    await_faces(faces, send_g, halo_g, g_sem, g_recv)


def ahead(counts, scale, act, f, g, weight):
    levels, channels, vox = f.shape
    depth = 9 * channels
    full = depth + -depth % 128
    vmem = pl.BlockSpec(memory_space=pltpu.VMEM)
    halo = (4, levels, channels, PLANE)
    return pl.pallas_call(
        functools.partial(ahead_kernel, counts, scale),
        out_shape=(
            jax.ShapeDtypeStruct(f.shape, jnp.bfloat16),
            jax.ShapeDtypeStruct((3, channels, depth), jnp.float32),
            jax.ShapeDtypeStruct((3 * channels, full), jnp.bfloat16),
            jax.ShapeDtypeStruct(halo, jnp.bfloat16),
        ),
        in_specs=[pl.BlockSpec(memory_space=pltpu.SMEM)] + [vmem] * 3,
        out_specs=(vmem,) * 4,
        scratch_shapes=[
            pltpu.VMEM((3 * channels, full), jnp.bfloat16),
            pltpu.VMEM(halo, jnp.bfloat16),
            pltpu.VMEM(halo, jnp.bfloat16),
            pltpu.VMEM(halo, jnp.bfloat16),
            pltpu.VMEM((levels, EDGE + 2, channels, PLANE), jnp.bfloat16),
            pltpu.VMEM((EDGE + 4, channels, PLANE), jnp.bfloat16),
            pltpu.VMEM((2, full, PLANE), jnp.bfloat16),
            pltpu.VMEM((2, channels, PLANE), jnp.float32),
            pltpu.VMEM((3 * channels, depth), jnp.float32),
        ]
        + [pltpu.SemaphoreType.DMA((4,))] * 4,
        compiler_params=pltpu.CompilerParams(
            collective_id=0, has_side_effects=True, vmem_limit_bytes=48 << 20
        ),
        cost_estimate=pl.CostEstimate(
            flops=levels * 4 * 27 * channels * channels * vox,
            bytes_accessed=8 * levels * channels * vox,
            transcendentals=0,
        ),
    )(act, f, g, weight)


def back_kernel(stages, act_ref, g_ref, halo_ref, w_ref, x_ref, gin_ref, sum_ref, *scratch):
    count = len(stages)
    acc, recv = scratch[: max(count - 1, 0)], scratch[max(count - 1, 0) : -5]
    cube, taps, carry, send_sem, recv_sem = scratch[-5:]
    levels, channels, _ = g_ref.shape
    here = {axis: lax.axis_index(axis) for axis in AXES}
    partners = []
    for axis, step in stages:
        bit = here[axis] // step % 2
        partners.append((bit, {axis: here[axis] + step - 2 * step * bit}))
    if count:
        barrier = pltpu.get_barrier_semaphore()
        for _bit, partner in partners:
            pl.semaphore_signal(barrier, inc=1, device_id=partner, device_id_type=MESH)
    sources = (x_ref,) + tuple(acc)

    def copy_of(stage):
        bit, partner = partners[stage]
        half = sources[stage].shape[0] // 2
        return pltpu.make_async_remote_copy(
            src_ref=sources[stage].at[pl.ds((1 - bit) * half, half)],
            dst_ref=recv[stage],
            send_sem=send_sem.at[stage],
            recv_sem=recv_sem.at[stage],
            device_id=partner,
            device_id_type=MESH,
        )

    def finish(stage):
        copy_of(stage).wait()
        half = sources[stage].shape[0] // 2
        bit = partners[stage][0]
        total = sources[stage][pl.ds(bit * half, half)] + recv[stage][...]
        if stage + 1 < count:
            acc[stage][...] = total
            copy_of(stage + 1).start()
        else:
            sum_ref[...] = total

    if count:
        pl.semaphore_wait(barrier, count)
        copy_of(0).start()
    else:
        sum_ref[...] = x_ref[...]

    lay_cube(act_ref, g_ref, cube)
    taps[...] = jnp.zeros_like(taps)
    pairs = EDGE // 2 + 1
    stops = [-(-levels * pairs * (i + 1) // (count + 1)) for i in range(count)]
    for level in range(levels):
        live = act_ref[0, level].astype(jnp.float32)
        carry[...] = jnp.zeros_like(carry)

        def build(at, slot):
            build_taps(level, levels, cube, halo_ref, taps, at, slot)

        def multiply(at, slot):
            add_plane(w_ref, live, level, taps, carry, gin_ref, at, slot)

        build(0, 0)
        at = 0
        for stage, stop in enumerate(stops):
            stop = stop - level * pairs
            if 0 < stop <= pairs:
                run_pairs(at, stop, build, multiply)
                at = stop
                finish(stage)
        if at < pairs:
            run_pairs(at, pairs, build, multiply)


def behind(stages, act, g, halo, w, parts):
    levels, channels, vox = g.shape
    vmem = pl.BlockSpec(memory_space=pltpu.VMEM)
    sizes = [parts.shape[0] >> (i + 1) for i in range(len(stages))]
    tail = parts.shape[1:]
    count = len(stages)
    return pl.pallas_call(
        functools.partial(back_kernel, stages),
        out_shape=(
            jax.ShapeDtypeStruct(g.shape, jnp.bfloat16),
            jax.ShapeDtypeStruct((parts.shape[0] >> count,) + tail, jnp.float32),
        ),
        in_specs=[pl.BlockSpec(memory_space=pltpu.SMEM)] + [vmem] * 4,
        out_specs=(vmem, vmem),
        scratch_shapes=[pltpu.VMEM((size,) + tail, jnp.float32) for size in sizes[:-1]]
        + [pltpu.VMEM((size,) + tail, jnp.float32) for size in sizes]
        + [
            pltpu.VMEM((levels, EDGE + 2, channels, PLANE), jnp.bfloat16),
            pltpu.VMEM((2, w.shape[1], PLANE), jnp.bfloat16),
            pltpu.VMEM((2, channels, PLANE), jnp.float32),
        ]
        + [pltpu.SemaphoreType.DMA((max(count, 1),))] * 2,
        compiler_params=pltpu.CompilerParams(
            collective_id=1 if count else None, has_side_effects=True, vmem_limit_bytes=48 << 20
        ),
        cost_estimate=pl.CostEstimate(
            flops=levels * 2 * 27 * channels * channels * vox,
            bytes_accessed=8 * levels * channels * vox,
            transcendentals=0,
        ),
    )(act, g, halo, w, parts)


def power_of_two(n):
    return n & (n - 1) == 0


def body(features, grad_out, weight, active):
    counts = [lax.axis_size(axis) for axis in AXES]
    levels, channels, vox = features.shape[2:]
    f, g, act = features[0, 0], grad_out[0, 0], active[0]
    scale = 1.0 / math.sqrt(counts[0] * counts[1] * levels * vox)
    out, gw, w_back, halo = ahead(counts, scale, act, f, g, weight)
    flat = gw.transpose(1, 0, 2).reshape(-1)
    devices = counts[0] * counts[1]
    chunk = flat.shape[0] // devices
    if devices > 1 and all(map(power_of_two, counts)) and chunk % 8 == 0:
        bits = [count.bit_length() - 1 for count in counts]
        total = sum(bits)
        order = [bits[0] - 1 - i for i in range(bits[0])] + [total - 1 - i for i in range(bits[1])]
        parts = flat.reshape((2,) * total + (8, chunk // 8))
        parts = parts.transpose(order + [total, total + 1]).reshape(devices, 8, chunk // 8)
        stages = [(AXES[a], 1 << i) for a in range(2) for i in range(bits[a])]
        gin, summed = behind(stages, act, g, halo, w_back, parts)
        summed = summed.reshape(chunk)
    else:
        gin, _ = behind([], act, g, halo, w_back, jnp.zeros((1, 8, 128), jnp.float32))
        summed = lax.psum_scatter(flat, AXES, scatter_dimension=0, tiled=True)
    return out[None, None], gin[None, None], summed


def solution(mesh):
    placed = (P("gx", "gy", None, None, None), P("gx", "gy", None, None, None), P(), P("gx", "gy", None))
    return jax.shard_map(
        body,
        mesh=mesh,
        in_specs=placed,
        out_specs=(
            P("gx", "gy", None, None, None),
            P("gx", "gy", None, None, None),
            P(("gx", "gy")),
        ),
        check_vma=False,
    )
```

profile of v0, /device:TPU:0, one launch (start us, length us, event | category | flops | bytes accessed | tf_op | source)
XLA Modules:
  0.0 69.6 jit_solution(15375478489735393550)
XLA Ops:
  0.6 0.0 copy-start
  0.6 1.4 %copy-done = bf16[1,1,2,96,4096]{4,3,2,1,0:T(8,128)(2,1)S(1)} copy-done((bf16[1,1,2,96,4096]{4,3,2,1,0:T(8,128)(2,1)S(1)}, bf16[1,1,2,96,4096]{4,3,2,1,0:T(8,128)(2,1)}, u32[]{:S(2)}) %copy-start) | copy-done | bytes 1572888
  2.0 0.0 copy-start.2
  2.0 1.0 %copy-done.2 = bf16[96,2592]{1,0:T(8,128)(2,1)S(1)} copy-done((bf16[96,2592]{1,0:T(8,128)(2,1)S(1)}, bf16[96,2592]{1,0:T(8,128)(2,1)}, u32[]{:S(2)}) %copy-start.2) | copy-done | bytes 497688
  3.1 0.0 copy-start.3
  3.1 0.7 copy-done.3
  3.7 28.5 %shard_map.67 = (bf16[2,96,4096]{2,1,0:T(8,128)(2,1)S(1)}, f32[3,96,864]{2,1,0:T(8,128)S(1)}, bf16[288,896]{1,0:T(8,128)(2,1)S(1)}, bf16[4,2,96,256]{3,2,1,0:T(8,128)(2,1)S(1)}) custom-call(s32[1,2]{1,0:T(1,128)S(1)} %bitcast.15, bf16[2,96,4096]{2,1,0:T(8,128)(2,1)S(1)} %bitcast.12, bf16[2,96,4096]{2,1,0:T(8,128)(2,1)} %bitcast.13, ...), custom_call_target="tpu_custom_call" | custom-call | flops 8153726976 | bytes 6291456 | tf_op jit(solution)/shard_map/pallas_call | solution.py:236
  32.3 0.0 copy-start.5
  32.3 0.8 %copy-done.5 = bf16[288,896]{1,0:T(8,128)(2,1)} copy-done((bf16[288,896]{1,0:T(8,128)(2,1)}, bf16[288,896]{1,0:T(8,128)(2,1)S(1)}, u32[]{:S(2)}) %copy-start.5) | copy-done | bytes 516120
  33.1 0.0 copy-start.7
  33.1 0.7 %copy-done.7 = bf16[4,2,96,256]{3,2,1,0:T(8,128)(2,1)} copy-done((bf16[4,2,96,256]{3,2,1,0:T(8,128)(2,1)}, bf16[4,2,96,256]{3,2,1,0:T(8,128)(2,1)S(1)}, u32[]{:S(2)}) %copy-start.7) | copy-done | bytes 393240
  33.8 0.7 %copy.7 = f32[96,3,864]{2,1,0:T(4,128)S(1)} copy(f32[96,3,864]{2,0,1:T(8,128)S(1)} %bitcast.11) | data formatting | bytes 1990656 | tf_op jit(solution)/shard_map/transpose | solution.py:383
  34.5 2.4 %reshape_reshape.3 = f32[2,2,2,2,2,8,972]{6,5,4,3,2,1,0:T(8,128)} reshape(f32[96,3,864]{2,1,0:T(4,128)S(1)} %copy.7) | data formatting | bytes 1990656 | tf_op jit(solution)/shard_map/reshape;reshape | solution.py:390
  36.9 0.0 copy-start.1
  36.9 0.0 copy-start.4
  36.9 0.0 copy-start.6
  37.0 1.5 %copy.8 = f32[2,2,2,2,2,8,972]{6,5,4,3,2,1,0:T(8,128)S(1)} copy(f32[2,2,2,2,2,8,972]{6,5,2,3,4,0,1:T(8,128)} %bitcast.17) | data formatting | bytes 1990656 | tf_op jit(solution)/shard_map/transpose | solution.py:391
  38.4 0.2 copy-done.1
  38.7 0.0 copy-done.4
  38.7 0.1 copy-done.6
  38.8 0.0 copy-start.8
  38.8 1.0 %copy-done.8 = bf16[4,2,96,256]{3,2,1,0:T(8,128)(2,1)S(1)} copy-done((bf16[4,2,96,256]{3,2,1,0:T(8,128)(2,1)S(1)}, bf16[4,2,96,256]{3,2,1,0:T(8,128)(2,1)}, u32[]{:S(2)}) %copy-start.8) | copy-done | bytes 393240
  39.8 26.8 %shard_map.68 = (bf16[2,96,4096]{2,1,0:T(8,128)(2,1)S(1)}, f32[1,8,972]{2,1,0:T(8,128)S(1)}) custom-call(s32[1,2]{1,0:T(1,128)S(1)} %bitcast.16, bf16[2,96,4096]{2,1,0:T(8,128)(2,1)S(1)} %bitcast.14, bf16[4,2,96,256]{3,2,1,0:T(8,128)(2,1)S(1)} %copy-done.8, bf16[288,896]{1,0:T(8,128)(2,1)S(1)} %copy-done.6, f32[32,8,972]{2,1,0:T(8,128)S(1)} %bitcast.10), custom_call_target="tpu_custom_call" | custom-call | flops 4076863488 | bytes 6291456 | tf_op jit(solution)/shard_map/pallas_call | solution.py:346
  66.6 0.7 %reshape.13 = f32[7776]{0:T(1024)} reshape(f32[1,8,972]{2,1,0:T(8,128)S(1)} %get-tuple-element.14) | data formatting | bytes 62208 | tf_op jit(solution)/shard_map/reshape | solution.py:394
  67.3 1.1 %copy.11 = bf16[1,1,2,96,4096]{4,3,2,1,0:T(8,128)(2,1)} copy(bf16[1,1,2,96,4096]{4,3,2,1,0:T(8,128)(2,1)S(1)} %bitcast.8) | data formatting | bytes 3145728
  68.5 1.1 %copy.12 = bf16[1,1,2,96,4096]{4,3,2,1,0:T(8,128)(2,1)} copy(bf16[1,1,2,96,4096]{4,3,2,1,0:T(8,128)(2,1)S(1)} %bitcast.9) | data formatting | bytes 3145728
Async XLA Ops:
  0.6 1.4 %copy-start = (bf16[1,1,2,96,4096]{4,3,2,1,0:T(8,128)(2,1)S(1)}, bf16[1,1,2,96,4096]{4,3,2,1,0:T(8,128)(2,1)}, u32[]{:S(2)}) copy-start(bf16[1,1,2,96,4096]{4,3,2,1,0:T(8,128)(2,1)} %param.4) | copy-start | bytes 4718596
  2.0 1.0 %copy-start.2 = (bf16[96,2592]{1,0:T(8,128)(2,1)S(1)}, bf16[96,2592]{1,0:T(8,128)(2,1)}, u32[]{:S(2)}) copy-start(bf16[96,2592]{1,0:T(8,128)(2,1)} %weight_ref.1) | copy-start | bytes 1492996
  3.1 0.7 copy-start.3
  32.3 0.8 %copy-start.5 = (bf16[288,896]{1,0:T(8,128)(2,1)}, bf16[288,896]{1,0:T(8,128)(2,1)S(1)}, u32[]{:S(2)}) copy-start(bf16[288,896]{1,0:T(8,128)(2,1)S(1)} %get-tuple-element.11.w_ref) | copy-start | bytes 1548292
  33.1 0.7 %copy-start.7 = (bf16[4,2,96,256]{3,2,1,0:T(8,128)(2,1)}, bf16[4,2,96,256]{3,2,1,0:T(8,128)(2,1)S(1)}, u32[]{:S(2)}) copy-start(bf16[4,2,96,256]{3,2,1,0:T(8,128)(2,1)S(1)} %get-tuple-element.10.halo_ref) | copy-start | bytes 1179652
  36.9 1.7 %copy-start.1 = (bf16[1,1,2,96,4096]{4,3,2,1,0:T(8,128)(2,1)S(1)}, bf16[1,1,2,96,4096]{4,3,2,1,0:T(8,128)(2,1)}, u32[]{:S(2)}) copy-start(bf16[1,1,2,96,4096]{4,3,2,1,0:T(8,128)(2,1)} %param.5) | copy-start | bytes 4718596
  36.9 1.7 %copy-start.4 = (s32[1,1,2]{2,1,0:T(1,128)S(1)}, s32[1,1,2]{2,1,0:T(1,128)}, u32[]{:S(2)}) copy-start(s32[1,1,2]{2,1,0:T(1,128)} %param.7) | copy-start | bytes 28
  36.9 1.8 %copy-start.6 = (bf16[288,896]{1,0:T(8,128)(2,1)S(1)}, bf16[288,896]{1,0:T(8,128)(2,1)}, u32[]{:S(2)}) copy-start(bf16[288,896]{1,0:T(8,128)(2,1)} %copy-done.5) | copy-start | bytes 1548292
  38.8 1.0 %copy-start.8 = (bf16[4,2,96,256]{3,2,1,0:T(8,128)(2,1)S(1)}, bf16[4,2,96,256]{3,2,1,0:T(8,128)(2,1)}, u32[]{:S(2)}) copy-start(bf16[4,2,96,256]{3,2,1,0:T(8,128)(2,1)} %copy-done.7) | copy-start | bytes 1179652
where the time goes:
time: 69.9 us; the launch traced here: 69.6 us
  Pallas kernels  55.4 us (79%)
  local copies, waits for them, and re-layouts  13.6 us (19%)
    pallas_call x1, Pallas kernels, ahead(): pl.pallas_call(functools.partial(ahead_kernel, counts, scale), out_shape=...  28.5 us
    pallas_call x1, Pallas kernels, behind(): pl.pallas_call(functools.partial(back_kernel, stages), out_shape=(jax.Sha...  26.8 us
    unnamed x20, local copies, waits for them, and re-layouts  8.26 us
    another operation x1, local copies, waits for them, and re-layouts, body(): parts = flat.reshape((2,) * total + (8, chunk // 8))  2.43 us
    transpose x1, local copies, waits for them, and re-layouts, body(): parts.transpose(order + [total, total + 1]).reshape(devices, 8, chunk // 8)  1.47 us

commit v1 on v0

--- a/solution.py
+++ b/solution.py
@@ -90,27 +90,14 @@
             cube[level, x + 1] = ref[level, :, x * PLANE : (x + 1) * PLANE] * live
 
 
-def build_taps(level, levels, cube, halo, taps, at, slot):
-    channels = cube.shape[2]
+def shift_nine(here, south, north, nears, taps, slot):
+    channels = here.shape[0]
     lane = lanes((channels, PLANE))
     y_at, z_at = lane // EDGE, lane % EDGE
-    at = jnp.asarray(at, jnp.int32)
 
     def roll(values, shift):
         return pltpu.roll(values, shift, 1)
 
-    inner = ((at >= 1) & (at <= EDGE)).astype(jnp.float32)
-    base = (at - 1) * EDGE
-    west = (at == 0).astype(jnp.bfloat16)
-    east = (at == EDGE + 1).astype(jnp.bfloat16)
-    here = cube[level, at] + halo[0, level] * west + halo[1, level] * east
-    here = here.astype(jnp.float32)
-    south = halo[2, level].astype(jnp.float32) * inner
-    north = halo[3, level].astype(jnp.float32) * inner
-    south = roll(south, (2 * PLANE - base) % PLANE)
-    north = roll(north, (2 * PLANE - EDGE - base) % PLANE)
-    nears = [cube[k, at].astype(jnp.float32) if 0 <= k < levels else None
-             for k in (level - 1, level + 1)]
     for dy in (-1, 0, 1):
         if dy < 0:
             moved = jnp.where(y_at == 0, south, roll(here, EDGE))
@@ -136,20 +123,41 @@
             taps[slot, pl.ds(tap * channels, channels), :] = value.astype(jnp.bfloat16)
 
 
+def near_planes(cube, level, at):
+    levels = cube.shape[0]
+    return [
+        cube[k, at].astype(jnp.float32) if 0 <= k < levels else None for k in (level - 1, level + 1)
+    ]
+
+
+def build_taps(level, cube, halo, taps, at, slot):
+    at = jnp.asarray(at, jnp.int32)
+    inner = ((at >= 1) & (at <= EDGE)).astype(jnp.float32)
+    base = (at - 1) * EDGE
+    west = (at == 0).astype(jnp.bfloat16)
+    east = (at == EDGE + 1).astype(jnp.bfloat16)
+    here = cube[level, at] + halo[0, level] * west + halo[1, level] * east
+    south = halo[2, level].astype(jnp.float32) * inner
+    north = halo[3, level].astype(jnp.float32) * inner
+    south = pltpu.roll(south, (2 * PLANE - base) % PLANE, 1)
+    north = pltpu.roll(north, (2 * PLANE - EDGE - base) % PLANE, 1)
+    shift_nine(here.astype(jnp.float32), south, north, near_planes(cube, level, at), taps, slot)
+
+
 def add_plane(w, live, level, taps, carry, ref, at, slot):
     channels = carry.shape[1]
     at = jnp.asarray(at, jnp.int32)
     target = pl.ds(pl.multiple_of(jnp.maximum(at - 2, 0) * PLANE, PLANE), PLANE)
-    y = jnp.dot(w[...], taps[slot], preferred_element_type=jnp.float32)
+    y = jnp.dot(w, taps[slot], preferred_element_type=jnp.float32)
     before, middle, after = (y[i * channels : (i + 1) * channels] for i in range(3))
     ref[level, :, target] = ((after + carry[0]) * live).astype(jnp.bfloat16)
     carry[0] = middle + carry[1]
     carry[1] = before
 
 
-def run_pairs(first, end, build, multiply):
+def run_pairs(first, end, build, multiply, base=0):
     def pair(i, unused):
-        at = 2 * i
+        at = base + 2 * i
         build(at + 1, 1)
         multiply(at, 0)
         build(jnp.minimum(at + 2, EDGE + 1), 0)
@@ -160,8 +168,8 @@
 
 
 def ahead_kernel(
-    counts, scale, act_ref, f_ref, g_ref, weight_ref, out_ref, gw_ref, w_back, halo_g,
-    w, halo_f, send_f, send_g, cube, own, taps, carry, gw, f_sem, f_recv, g_sem, g_recv,
+    counts, scale, act_ref, f_ref, g_ref, gw_ref, halo_f, halo_g,
+    send_f, send_g, cube, own, taps, gw, edges, f_sem, f_recv, g_sem, g_recv,
 ):
     levels, channels, _ = f_ref.shape
     depth = 9 * channels
@@ -179,97 +187,113 @@
     fill_faces(act_ref, g_ref, send_g)
     send_faces(faces, send_g, halo_g, g_sem, g_recv)
 
-    wide = weight_ref[...].astype(jnp.float32)
-    w[...] = jnp.zeros_like(w)
-    w_back[...] = jnp.zeros_like(w_back)
-    for dx in range(3):
-        rows = slice(dx * channels, (dx + 1) * channels)
-        w[rows, :depth] = wide[:, dx * depth : (dx + 1) * depth].astype(jnp.bfloat16)
-        blocks = []
-        for tap in range(9):
-            start = ((2 - dx) * 9 + 8 - tap) * channels
-            blocks.append(wide[:, start : start + channels].T)
-        w_back[rows, :depth] = jnp.concatenate(blocks, axis=1).astype(jnp.bfloat16)
-
     lay_cube(act_ref, f_ref, cube)
-    taps[...] = jnp.zeros_like(taps)
     gw[...] = jnp.zeros_like(gw)
     zero = jnp.zeros((channels, PLANE), jnp.bfloat16)
-    for at in (0, 1, EDGE + 2, EDGE + 3):
-        own[at] = zero
+    for level in range(levels):
+        live = act_ref[0, level].astype(jnp.bfloat16)
+        for at in (0, 1, EDGE + 2, EDGE + 3):
+            own[level, at] = zero
+        for x in range(EDGE):
+            own[level, x + 2] = g_ref[level, :, x * PLANE : (x + 1) * PLANE] * live
+
+    def product(left, slot):
+        return lax.dot_general(
+            left, taps[slot], (((1,), (1,)), ((), ())), preferred_element_type=jnp.float32
+        )
+
+    for level in range(levels):
+
+        def build(at, slot):
+            here = cube[level, at].astype(jnp.float32)
+            shift_nine(here, 0.0, 0.0, near_planes(cube, level, at), taps, slot)
+
+        def multiply(at, slot):
+            gw[...] += product(own[level, pl.ds(at, 3)].reshape(3 * channels, PLANE), slot)
+
+        build(1, 0)
+        run_pairs(0, EDGE // 2, build, multiply, 1)
+
     await_faces(faces, send_f, halo_f, f_sem, f_recv)
-
-    for level in range(levels):
-        live = act_ref[0, level]
-        for x in range(EDGE):
-            plane = g_ref[level, :, x * PLANE : (x + 1) * PLANE]
-            own[x + 2] = plane * live.astype(jnp.bfloat16)
-        carry[...] = jnp.zeros_like(carry)
-
-        def build(at, slot):
-            build_taps(level, levels, cube, halo_f, taps, at, slot)
-
-        def multiply(at, slot):
-            add_plane(w, live.astype(jnp.float32), level, taps, carry, out_ref, at, slot)
-            grads = own[pl.ds(at, 3)].reshape(3 * channels, PLANE)
-            gw[...] += lax.dot_general(
-                grads,
-                taps[slot, :depth, :],
-                (((1,), (1,)), ((), ())),
-                preferred_element_type=jnp.float32,
-            )
-
-        build(0, 0)
-        run_pairs(0, EDGE // 2 + 1, build, multiply)
-
+    for level in range(levels):
+        for slot, at in enumerate((0, EDGE + 1)):
+            here = halo_f[slot, level].astype(jnp.float32)
+            shift_nine(here, 0.0, 0.0, (None, None), taps, slot)
+            gw[...] += product(own[level, pl.ds(at, 3)].reshape(3 * channels, PLANE), slot)
+        for slot in range(2):
+            here = halo_f[2 + slot, level].astype(jnp.float32)
+            shift_nine(here, 0.0, 0.0, (None, None), taps, slot)
+            term = product(send_g[2 + slot, level], slot)
+            edges[slot] = edges[slot] + term if level else term
+
+    third = depth // 3
     for dx in range(3):
-        gw_ref[dx] = gw[(2 - dx) * channels : (3 - dx) * channels, :] * scale
+        part = slice(dx * third, (dx + 1) * third)
+        rows = gw[(2 - dx) * channels : (3 - dx) * channels, :]
+        south = rows[:, :third] + edges[0][:, part]
+        north = rows[:, 2 * third :] + edges[1][:, part]
+        joined = jnp.concatenate([south, rows[:, third : 2 * third], north], axis=1)
+        gw_ref[dx] = joined * scale
     await_faces(faces, send_g, halo_g, g_sem, g_recv)
 
 
-def ahead(counts, scale, act, f, g, weight):
+def ahead(counts, scale, act, f, g):
     levels, channels, vox = f.shape
     depth = 9 * channels
-    full = depth + -depth % 128
     vmem = pl.BlockSpec(memory_space=pltpu.VMEM)
     halo = (4, levels, channels, PLANE)
     return pl.pallas_call(
         functools.partial(ahead_kernel, counts, scale),
         out_shape=(
-            jax.ShapeDtypeStruct(f.shape, jnp.bfloat16),
             jax.ShapeDtypeStruct((3, channels, depth), jnp.float32),
-            jax.ShapeDtypeStruct((3 * channels, full), jnp.bfloat16),
             jax.ShapeDtypeStruct(halo, jnp.bfloat16),
-        ),
-        in_specs=[pl.BlockSpec(memory_space=pltpu.SMEM)] + [vmem] * 3,
-        out_specs=(vmem,) * 4,
+            jax.ShapeDtypeStruct(halo, jnp.bfloat16),
+        ),
+        in_specs=[pl.BlockSpec(memory_space=pltpu.SMEM)] + [vmem] * 2,
+        out_specs=(vmem,) * 3,
         scratch_shapes=[
-            pltpu.VMEM((3 * channels, full), jnp.bfloat16),
-            pltpu.VMEM(halo, jnp.bfloat16),
             pltpu.VMEM(halo, jnp.bfloat16),
             pltpu.VMEM(halo, jnp.bfloat16),
             pltpu.VMEM((levels, EDGE + 2, channels, PLANE), jnp.bfloat16),
-            pltpu.VMEM((EDGE + 4, channels, PLANE), jnp.bfloat16),
-            pltpu.VMEM((2, full, PLANE), jnp.bfloat16),
-            pltpu.VMEM((2, channels, PLANE), jnp.float32),
+            pltpu.VMEM((levels, EDGE + 4, channels, PLANE), jnp.bfloat16),
+            pltpu.VMEM((2, depth, PLANE), jnp.bfloat16),
             pltpu.VMEM((3 * channels, depth), jnp.float32),
+            pltpu.VMEM((2, channels, depth), jnp.float32),
         ]
         + [pltpu.SemaphoreType.DMA((4,))] * 4,
         compiler_params=pltpu.CompilerParams(
             collective_id=0, has_side_effects=True, vmem_limit_bytes=48 << 20
         ),
         cost_estimate=pl.CostEstimate(
-            flops=levels * 4 * 27 * channels * channels * vox,
+            flops=levels * 2 * 27 * channels * channels * vox,
             bytes_accessed=8 * levels * channels * vox,
             transcendentals=0,
         ),
-    )(act, f, g, weight)
-
-
-def back_kernel(stages, act_ref, g_ref, halo_ref, w_ref, x_ref, gin_ref, sum_ref, *scratch):
+    )(act, f, g)
+
+
+def lay_weights(weight_ref, w):
+    channels = weight_ref.shape[0]
+    depth = 9 * channels
+    wide = weight_ref[...].astype(jnp.float32)
+    w[...] = jnp.zeros_like(w)
+    for dx in range(3):
+        rows = slice(dx * channels, (dx + 1) * channels)
+        w[0, rows, :depth] = wide[:, dx * depth : (dx + 1) * depth].astype(jnp.bfloat16)
+        blocks = []
+        for tap in range(9):
+            start = ((2 - dx) * 9 + 8 - tap) * channels
+            blocks.append(wide[:, start : start + channels].T)
+        w[1, rows, :depth] = jnp.concatenate(blocks, axis=1).astype(jnp.bfloat16)
+
+
+def back_kernel(
+    stages, act_ref, f_ref, g_ref, halo_f, halo_g, weight_ref, x_ref, out_ref, gin_ref, sum_ref,
+    *scratch,
+):
     count = len(stages)
-    acc, recv = scratch[: max(count - 1, 0)], scratch[max(count - 1, 0) : -5]
-    cube, taps, carry, send_sem, recv_sem = scratch[-5:]
+    acc, recv = scratch[: max(count - 1, 0)], scratch[max(count - 1, 0) : -6]
+    cube, taps, carry, w, send_sem, recv_sem = scratch[-6:]
     levels, channels, _ = g_ref.shape
     here = {axis: lax.axis_index(axis) for axis in AXES}
     partners = []
@@ -311,19 +335,25 @@
     else:
         sum_ref[...] = x_ref[...]
 
-    lay_cube(act_ref, g_ref, cube)
+    lay_weights(weight_ref, w)
     taps[...] = jnp.zeros_like(taps)
+    lay_cube(act_ref, f_ref, cube.at[0])
+    lay_cube(act_ref, g_ref, cube.at[1])
     pairs = EDGE // 2 + 1
-    stops = [-(-levels * pairs * (i + 1) // (count + 1)) for i in range(count)]
+    lengths = [1.2 + 5 * 0.5 ** (i - 1) if i else 2.0 for i in range(count)]
+    stops = [round(levels * pairs * sum(lengths[: i + 1]) / sum(lengths)) for i in range(count)]
     for level in range(levels):
         live = act_ref[0, level].astype(jnp.float32)
         carry[...] = jnp.zeros_like(carry)
+        work = ((halo_f, out_ref), (halo_g, gin_ref))
 
         def build(at, slot):
-            build_taps(level, levels, cube, halo_ref, taps, at, slot)
+            for k, (halo, _ref) in enumerate(work):
+                build_taps(level, cube.at[k], halo, taps.at[k], at, slot)
 
         def multiply(at, slot):
-            add_plane(w_ref, live, level, taps, carry, gin_ref, at, slot)
+            for k, (_halo, ref) in enumerate(work):
+                add_plane(w[k], live, level, taps.at[k], carry.at[k], ref, at, slot)
 
         build(0, 0)
         at = 0
@@ -337,8 +367,9 @@
             run_pairs(at, pairs, build, multiply)
 
 
-def behind(stages, act, g, halo, w, parts):
+def behind(stages, act, f, g, halo_f, halo_g, weight, parts):
     levels, channels, vox = g.shape
+    full = 9 * channels + -9 * channels % 128
     vmem = pl.BlockSpec(memory_space=pltpu.VMEM)
     sizes = [parts.shape[0] >> (i + 1) for i in range(len(stages))]
     tail = parts.shape[1:]
@@ -346,28 +377,30 @@
     return pl.pallas_call(
         functools.partial(back_kernel, stages),
         out_shape=(
+            jax.ShapeDtypeStruct(f.shape, jnp.bfloat16),
             jax.ShapeDtypeStruct(g.shape, jnp.bfloat16),
             jax.ShapeDtypeStruct((parts.shape[0] >> count,) + tail, jnp.float32),
         ),
-        in_specs=[pl.BlockSpec(memory_space=pltpu.SMEM)] + [vmem] * 4,
-        out_specs=(vmem, vmem),
+        in_specs=[pl.BlockSpec(memory_space=pltpu.SMEM)] + [vmem] * 6,
+        out_specs=(vmem, vmem, vmem),
         scratch_shapes=[pltpu.VMEM((size,) + tail, jnp.float32) for size in sizes[:-1]]
         + [pltpu.VMEM((size,) + tail, jnp.float32) for size in sizes]
         + [
-            pltpu.VMEM((levels, EDGE + 2, channels, PLANE), jnp.bfloat16),
-            pltpu.VMEM((2, w.shape[1], PLANE), jnp.bfloat16),
-            pltpu.VMEM((2, channels, PLANE), jnp.float32),
+            pltpu.VMEM((2, levels, EDGE + 2, channels, PLANE), jnp.bfloat16),
+            pltpu.VMEM((2, 2, full, PLANE), jnp.bfloat16),
+            pltpu.VMEM((2, 2, channels, PLANE), jnp.float32),
+            pltpu.VMEM((2, 3 * channels, full), jnp.bfloat16),
         ]
         + [pltpu.SemaphoreType.DMA((max(count, 1),))] * 2,
         compiler_params=pltpu.CompilerParams(
             collective_id=1 if count else None, has_side_effects=True, vmem_limit_bytes=48 << 20
         ),
         cost_estimate=pl.CostEstimate(
-            flops=levels * 2 * 27 * channels * channels * vox,
-            bytes_accessed=8 * levels * channels * vox,
+            flops=levels * 4 * 27 * channels * channels * vox,
+            bytes_accessed=16 * levels * channels * vox,
             transcendentals=0,
         ),
-    )(act, g, halo, w, parts)
+    )(act, f, g, halo_f, halo_g, weight, parts)
 
 
 def power_of_two(n):
@@ -379,7 +412,8 @@
     levels, channels, vox = features.shape[2:]
     f, g, act = features[0, 0], grad_out[0, 0], active[0]
     scale = 1.0 / math.sqrt(counts[0] * counts[1] * levels * vox)
-    out, gw, w_back, halo = ahead(counts, scale, act, f, g, weight)
+    gw, halo_f, halo_g = ahead(counts, scale, act, f, g)
+    operands = (act, f, g, halo_f, halo_g, weight)
     flat = gw.transpose(1, 0, 2).reshape(-1)
     devices = counts[0] * counts[1]
     chunk = flat.shape[0] // devices
@@ -390,10 +424,10 @@
         parts = flat.reshape((2,) * total + (8, chunk // 8))
         parts = parts.transpose(order + [total, total + 1]).reshape(devices, 8, chunk // 8)
         stages = [(AXES[a], 1 << i) for a in range(2) for i in range(bits[a])]
-        gin, summed = behind(stages, act, g, halo, w_back, parts)
+        out, gin, summed = behind(stages, *operands, parts)
         summed = summed.reshape(chunk)
     else:
-        gin, _ = behind([], act, g, halo, w_back, jnp.zeros((1, 8, 128), jnp.float32))
+        out, gin, _ = behind([], *operands, jnp.zeros((1, 8, 128), jnp.float32))
         summed = lax.psum_scatter(flat, AXES, scatter_dimension=0, tiled=True)
     return out[None, None], gin[None, None], summed
 

time: 69.9 us -> 63.6 us (0.910)
  Pallas kernels: 55.4 us -> 51.3 us
  local copies, waits for them, and re-layouts: 13.6 us -> 11.3 us
    pallas_call x1, Pallas kernels: 28.5 us -> 19.1 us  [ahead(): pl.pallas_call(functools.partial(ahead_kernel, counts, scale), out_shape=...]
    pallas_call x1, Pallas kernels: 26.8 us -> 32.2 us  [behind(): pl.pallas_call(functools.partial(back_kernel, stages), out_shape=(jax.Sha...]
    transpose x1, local copies, waits for them, and re-layouts: 1.47 us -> 0.07 us  [body(): parts.transpose(order + [total, total + 1]).reshape(devices, 8, chunk // 8)]
    another operation x1, local copies, waits for them, and re-layouts: 2.43 us -> 1.45 us  [body(): parts = flat.reshape((2,) * total + (8, chunk // 8))]
where the time goes in v1:
time: 63.6 us; the launch traced here: 63.4 us
  Pallas kernels  51.3 us (81%)
  local copies, waits for them, and re-layouts  11.3 us (18%)
  between operations  0.72 us (1%)
    pallas_call x1, Pallas kernels, behind(): pl.pallas_call(functools.partial(back_kernel, stages), out_shape=(jax.Sha...  32.2 us
    pallas_call x1, Pallas kernels, ahead(): pl.pallas_call(functools.partial(ahead_kernel, counts, scale), out_shape=...  19.1 us
    unnamed x20, local copies, waits for them, and re-layouts  8.42 us
    another operation x1, local copies, waits for them, and re-layouts, body(): parts = flat.reshape((2,) * total + (8, chunk // 8))  1.45 us

profile of v1, /device:TPU:0, one launch (start us, length us, event | category | flops | bytes accessed | tf_op | source)
XLA Modules:
  0.0 63.4 jit_solution(11445280874758334767)
XLA Ops:
  0.6 0.0 copy-start
  0.6 1.4 %copy-done = bf16[1,1,2,96,4096]{4,3,2,1,0:T(8,128)(2,1)S(1)} copy-done((bf16[1,1,2,96,4096]{4,3,2,1,0:T(8,128)(2,1)S(1)}, bf16[1,1,2,96,4096]{4,3,2,1,0:T(8,128)(2,1)}, u32[]{:S(2)}) %copy-start) | copy-done | bytes 1572888
  2.0 0.0 copy-start.1
  2.0 1.4 %copy-done.1 = bf16[1,1,2,96,4096]{4,3,2,1,0:T(8,128)(2,1)S(1)} copy-done((bf16[1,1,2,96,4096]{4,3,2,1,0:T(8,128)(2,1)S(1)}, bf16[1,1,2,96,4096]{4,3,2,1,0:T(8,128)(2,1)}, u32[]{:S(2)}) %copy-start.1) | copy-done | bytes 1572888
  3.4 0.0 copy-start.3
  3.5 0.7 %copy-done.3 = s32[1,1,2]{2,1,0:T(1,128)S(1)} copy-done((s32[1,1,2]{2,1,0:T(1,128)S(1)}, s32[1,1,2]{2,1,0:T(1,128)}, u32[]{:S(2)}) %copy-start.3) | copy-done | bytes 32
  4.1 19.1 %shard_map.67 = (f32[3,96,864]{2,1,0:T(8,128)S(1)}, bf16[4,2,96,256]{3,2,1,0:T(8,128)(2,1)S(1)}, bf16[4,2,96,256]{3,2,1,0:T(8,128)(2,1)S(1)}) custom-call(s32[1,2]{1,0:T(1,128)S(1)} %bitcast.16, bf16[2,96,4096]{2,1,0:T(8,128)(2,1)S(1)} %bitcast.13, bf16[2,96,4096]{2,1,0:T(8,128)(2,1)S(1)} %bitcast.15), custom_call_target="tpu_custom_call" | custom-call | flops 4076863488 | bytes 6291456 | tf_op jit(solution)/shard_map/pallas_call | solution.py:245
  23.2 0.0 copy-start.5
  23.2 0.7 %copy-done.5 = bf16[4,2,96,256]{3,2,1,0:T(8,128)(2,1)} copy-done((bf16[4,2,96,256]{3,2,1,0:T(8,128)(2,1)}, bf16[4,2,96,256]{3,2,1,0:T(8,128)(2,1)S(1)}, u32[]{:S(2)}) %copy-start.5) | copy-done | bytes 393240
  24.0 0.0 copy-start.7
  24.0 0.7 %copy-done.7 = bf16[4,2,96,256]{3,2,1,0:T(8,128)(2,1)} copy-done((bf16[4,2,96,256]{3,2,1,0:T(8,128)(2,1)}, bf16[4,2,96,256]{3,2,1,0:T(8,128)(2,1)S(1)}, u32[]{:S(2)}) %copy-start.7) | copy-done | bytes 393240
  24.7 0.7 %copy.7 = f32[96,3,864]{2,1,0:T(4,128)S(1)} copy(f32[96,3,864]{2,0,1:T(8,128)S(1)} %bitcast.11) | data formatting | bytes 1990656 | tf_op jit(solution)/shard_map/transpose | solution.py:417
  25.4 1.4 %reshape_reshape.3 = f32[2,2,2,2,2,8,972]{6,5,4,3,2,1,0:T(8,128)S(1)} reshape(f32[96,3,864]{2,1,0:T(4,128)S(1)} %copy.7) | data formatting | bytes 1990656 | tf_op jit(solution)/shard_map/reshape;reshape | solution.py:424
  26.9 0.0 copy-start.2
  26.9 0.0 copy-start.4
  26.9 0.0 copy-start.6
  26.9 0.0 copy-start.8
  26.9 0.1 copy.8
  27.0 0.9 %copy-done.2 = bf16[96,2592]{1,0:T(8,128)(2,1)S(1)} copy-done((bf16[96,2592]{1,0:T(8,128)(2,1)S(1)}, bf16[96,2592]{1,0:T(8,128)(2,1)}, u32[]{:S(2)}) %copy-start.2) | copy-done | bytes 497688
  27.9 0.0 copy-done.4
  27.9 0.1 copy-done.6
  28.1 0.1 copy-done.8
  28.2 32.2 %shard_map.68 = (bf16[2,96,4096]{2,1,0:T(8,128)(2,1)S(1)}, bf16[2,96,4096]{2,1,0:T(8,128)(2,1)S(1)}, f32[1,8,972]{2,1,0:T(8,128)S(1)}) custom-call(s32[1,2]{1,0:T(1,128)S(1)} %bitcast.17, bf16[2,96,4096]{2,1,0:T(8,128)(2,1)} %bitcast.12, bf16[2,96,4096]{2,1,0:T(8,128)(2,1)} %bitcast.14, bf16[4,2,96,256]{3,2,1,0:T(8,128)(2,1)S(1)} %copy-done.6, ...), custom_call_target="tpu_custom_call" | custom-call | flops 8153726976 | bytes 12582912 | tf_op jit(solution)/shard_map/pallas_call | solution.py:377
  60.4 0.7 %reshape.13 = f32[7776]{0:T(1024)} reshape(f32[1,8,972]{2,1,0:T(8,128)S(1)} %get-tuple-element.14) | data formatting | bytes 62208 | tf_op jit(solution)/shard_map/reshape | solution.py:428
  61.1 1.1 %copy.11 = bf16[1,1,2,96,4096]{4,3,2,1,0:T(8,128)(2,1)} copy(bf16[1,1,2,96,4096]{4,3,2,1,0:T(8,128)(2,1)S(1)} %bitcast.9) | data formatting | bytes 3145728
  62.3 1.1 %copy.12 = bf16[1,1,2,96,4096]{4,3,2,1,0:T(8,128)(2,1)} copy(bf16[1,1,2,96,4096]{4,3,2,1,0:T(8,128)(2,1)S(1)} %bitcast.8) | data formatting | bytes 3145728
Async XLA Ops:
  0.6 1.4 %copy-start = (bf16[1,1,2,96,4096]{4,3,2,1,0:T(8,128)(2,1)S(1)}, bf16[1,1,2,96,4096]{4,3,2,1,0:T(8,128)(2,1)}, u32[]{:S(2)}) copy-start(bf16[1,1,2,96,4096]{4,3,2,1,0:T(8,128)(2,1)} %param.4) | copy-start | bytes 4718596
  2.0 1.4 %copy-start.1 = (bf16[1,1,2,96,4096]{4,3,2,1,0:T(8,128)(2,1)S(1)}, bf16[1,1,2,96,4096]{4,3,2,1,0:T(8,128)(2,1)}, u32[]{:S(2)}) copy-start(bf16[1,1,2,96,4096]{4,3,2,1,0:T(8,128)(2,1)} %param.5) | copy-start | bytes 4718596
  3.4 0.7 %copy-start.3 = (s32[1,1,2]{2,1,0:T(1,128)S(1)}, s32[1,1,2]{2,1,0:T(1,128)}, u32[]{:S(2)}) copy-start(s32[1,1,2]{2,1,0:T(1,128)} %param.7) | copy-start | bytes 28
  23.2 0.7 %copy-start.5 = (bf16[4,2,96,256]{3,2,1,0:T(8,128)(2,1)}, bf16[4,2,96,256]{3,2,1,0:T(8,128)(2,1)S(1)}, u32[]{:S(2)}) copy-start(bf16[4,2,96,256]{3,2,1,0:T(8,128)(2,1)S(1)} %get-tuple-element.9.halo_f) | copy-start | bytes 1179652
  24.0 0.7 %copy-start.7 = (bf16[4,2,96,256]{3,2,1,0:T(8,128)(2,1)}, bf16[4,2,96,256]{3,2,1,0:T(8,128)(2,1)S(1)}, u32[]{:S(2)}) copy-start(bf16[4,2,96,256]{3,2,1,0:T(8,128)(2,1)S(1)} %get-tuple-element.10.halo_g) | copy-start | bytes 1179652
  26.9 1.0 %copy-start.2 = (bf16[96,2592]{1,0:T(8,128)(2,1)S(1)}, bf16[96,2592]{1,0:T(8,128)(2,1)}, u32[]{:S(2)}) copy-start(bf16[96,2592]{1,0:T(8,128)(2,1)} %weight_ref.1) | copy-start | bytes 1492996
  26.9 1.0 %copy-start.4 = (s32[1,1,2]{2,1,0:T(1,128)S(1)}, s32[1,1,2]{2,1,0:T(1,128)}, u32[]{:S(2)}) copy-start(s32[1,1,2]{2,1,0:T(1,128)} %param.7) | copy-start | bytes 28
  26.9 1.1 %copy-start.6 = (bf16[4,2,96,256]{3,2,1,0:T(8,128)(2,1)S(1)}, bf16[4,2,96,256]{3,2,1,0:T(8,128)(2,1)}, u32[]{:S(2)}) copy-start(bf16[4,2,96,256]{3,2,1,0:T(8,128)(2,1)} %copy-done.5) | copy-start | bytes 1179652
  26.9 1.3 %copy-start.8 = (bf16[4,2,96,256]{3,2,1,0:T(8,128)(2,1)S(1)}, bf16[4,2,96,256]{3,2,1,0:T(8,128)(2,1)}, u32[]{:S(2)}) copy-start(bf16[4,2,96,256]{3,2,1,0:T(8,128)(2,1)} %copy-done.7) | copy-start | bytes 1179652

commit v2 on v1

--- a/solution.py
+++ b/solution.py
@@ -341,7 +341,7 @@
     lay_cube(act_ref, g_ref, cube.at[1])
     pairs = EDGE // 2 + 1
     lengths = [1.2 + 5 * 0.5 ** (i - 1) if i else 2.0 for i in range(count)]
-    stops = [round(levels * pairs * sum(lengths[: i + 1]) / sum(lengths)) for i in range(count)]
+    stops = [round(0.8 * levels * pairs * sum(lengths[: i + 1]) / sum(lengths)) for i in range(count)]
     for level in range(levels):
         live = act_ref[0, level].astype(jnp.float32)
         carry[...] = jnp.zeros_like(carry)

time: 63.6 us -> 66.4 us (1.044)
  Pallas kernels: 51.3 us -> 54.1 us
    pallas_call x1, Pallas kernels: 32.2 us -> 35 us  [behind(): pl.pallas_call(functools.partial(back_kernel, stages), out_shape=(jax.Sha...]
where the time goes in v2:
time: 66.4 us; the launch traced here: 66.2 us
  Pallas kernels  54.1 us (81%)
  local copies, waits for them, and re-layouts  11.3 us (17%)
  between operations  0.72 us (1%)
    pallas_call x1, Pallas kernels, behind(): pl.pallas_call(functools.partial(back_kernel, stages), out_shape=(jax.Sha...  35 us
    pallas_call x1, Pallas kernels, ahead(): pl.pallas_call(functools.partial(ahead_kernel, counts, scale), out_shape=...  19.1 us
    unnamed x20, local copies, waits for them, and re-layouts  8.42 us
    another operation x1, local copies, waits for them, and re-layouts, body(): parts = flat.reshape((2,) * total + (8, chunk // 8))  1.45 us

profile of v2, /device:TPU:0, one launch (start us, length us, event | category | flops | bytes accessed | tf_op | source)
XLA Modules:
  0.0 66.2 jit_solution(4701873360416694332)
XLA Ops:
  0.6 0.0 copy-start
  0.6 1.4 %copy-done = bf16[1,1,2,96,4096]{4,3,2,1,0:T(8,128)(2,1)S(1)} copy-done((bf16[1,1,2,96,4096]{4,3,2,1,0:T(8,128)(2,1)S(1)}, bf16[1,1,2,96,4096]{4,3,2,1,0:T(8,128)(2,1)}, u32[]{:S(2)}) %copy-start) | copy-done | bytes 1572888
  2.0 0.0 copy-start.1
  2.0 1.4 %copy-done.1 = bf16[1,1,2,96,4096]{4,3,2,1,0:T(8,128)(2,1)S(1)} copy-done((bf16[1,1,2,96,4096]{4,3,2,1,0:T(8,128)(2,1)S(1)}, bf16[1,1,2,96,4096]{4,3,2,1,0:T(8,128)(2,1)}, u32[]{:S(2)}) %copy-start.1) | copy-done | bytes 1572888
  3.4 0.0 copy-start.3
  3.5 0.7 copy-done.3
  4.1 19.1 %shard_map.67 = (f32[3,96,864]{2,1,0:T(8,128)S(1)}, bf16[4,2,96,256]{3,2,1,0:T(8,128)(2,1)S(1)}, bf16[4,2,96,256]{3,2,1,0:T(8,128)(2,1)S(1)}) custom-call(s32[1,2]{1,0:T(1,128)S(1)} %bitcast.16, bf16[2,96,4096]{2,1,0:T(8,128)(2,1)S(1)} %bitcast.13, bf16[2,96,4096]{2,1,0:T(8,128)(2,1)S(1)} %bitcast.15), custom_call_target="tpu_custom_call" | custom-call | flops 4076863488 | bytes 6291456 | tf_op jit(solution)/shard_map/pallas_call | solution.py:245
  23.2 0.0 copy-start.5
  23.2 0.7 %copy-done.5 = bf16[4,2,96,256]{3,2,1,0:T(8,128)(2,1)} copy-done((bf16[4,2,96,256]{3,2,1,0:T(8,128)(2,1)}, bf16[4,2,96,256]{3,2,1,0:T(8,128)(2,1)S(1)}, u32[]{:S(2)}) %copy-start.5) | copy-done | bytes 393240
  24.0 0.0 copy-start.7
  24.0 0.7 %copy-done.7 = bf16[4,2,96,256]{3,2,1,0:T(8,128)(2,1)} copy-done((bf16[4,2,96,256]{3,2,1,0:T(8,128)(2,1)}, bf16[4,2,96,256]{3,2,1,0:T(8,128)(2,1)S(1)}, u32[]{:S(2)}) %copy-start.7) | copy-done | bytes 393240
  24.7 0.7 %copy.7 = f32[96,3,864]{2,1,0:T(4,128)S(1)} copy(f32[96,3,864]{2,0,1:T(8,128)S(1)} %bitcast.11) | data formatting | bytes 1990656 | tf_op jit(solution)/shard_map/transpose | solution.py:417
  25.4 1.4 %reshape_reshape.3 = f32[2,2,2,2,2,8,972]{6,5,4,3,2,1,0:T(8,128)S(1)} reshape(f32[96,3,864]{2,1,0:T(4,128)S(1)} %copy.7) | data formatting | bytes 1990656 | tf_op jit(solution)/shard_map/reshape;reshape | solution.py:424
  26.9 0.0 copy-start.2
  26.9 0.0 copy-start.4
  26.9 0.0 copy-start.6
  26.9 0.0 copy-start.8
  26.9 0.1 copy.8
  27.0 0.9 %copy-done.2 = bf16[96,2592]{1,0:T(8,128)(2,1)S(1)} copy-done((bf16[96,2592]{1,0:T(8,128)(2,1)S(1)}, bf16[96,2592]{1,0:T(8,128)(2,1)}, u32[]{:S(2)}) %copy-start.2) | copy-done | bytes 497688
  27.9 0.0 copy-done.4
  27.9 0.1 copy-done.6
  28.1 0.1 copy-done.8
  28.2 35.0 %shard_map.68 = (bf16[2,96,4096]{2,1,0:T(8,128)(2,1)S(1)}, bf16[2,96,4096]{2,1,0:T(8,128)(2,1)S(1)}, f32[1,8,972]{2,1,0:T(8,128)S(1)}) custom-call(s32[1,2]{1,0:T(1,128)S(1)} %bitcast.17, bf16[2,96,4096]{2,1,0:T(8,128)(2,1)} %bitcast.12, bf16[2,96,4096]{2,1,0:T(8,128)(2,1)} %bitcast.14, bf16[4,2,96,256]{3,2,1,0:T(8,128)(2,1)S(1)} %copy-done.6, ...), custom_call_target="tpu_custom_call" | custom-call | flops 8153726976 | bytes 12582912 | tf_op jit(solution)/shard_map/pallas_call | solution.py:377
  63.2 0.7 %reshape.13 = f32[7776]{0:T(1024)} reshape(f32[1,8,972]{2,1,0:T(8,128)S(1)} %get-tuple-element.14) | data formatting | bytes 62208 | tf_op jit(solution)/shard_map/reshape | solution.py:428
  63.9 1.1 %copy.11 = bf16[1,1,2,96,4096]{4,3,2,1,0:T(8,128)(2,1)} copy(bf16[1,1,2,96,4096]{4,3,2,1,0:T(8,128)(2,1)S(1)} %bitcast.9) | data formatting | bytes 3145728
  65.1 1.1 %copy.12 = bf16[1,1,2,96,4096]{4,3,2,1,0:T(8,128)(2,1)} copy(bf16[1,1,2,96,4096]{4,3,2,1,0:T(8,128)(2,1)S(1)} %bitcast.8) | data formatting | bytes 3145728
Async XLA Ops:
  0.6 1.4 %copy-start = (bf16[1,1,2,96,4096]{4,3,2,1,0:T(8,128)(2,1)S(1)}, bf16[1,1,2,96,4096]{4,3,2,1,0:T(8,128)(2,1)}, u32[]{:S(2)}) copy-start(bf16[1,1,2,96,4096]{4,3,2,1,0:T(8,128)(2,1)} %param.4) | copy-start | bytes 4718596
  2.0 1.4 %copy-start.1 = (bf16[1,1,2,96,4096]{4,3,2,1,0:T(8,128)(2,1)S(1)}, bf16[1,1,2,96,4096]{4,3,2,1,0:T(8,128)(2,1)}, u32[]{:S(2)}) copy-start(bf16[1,1,2,96,4096]{4,3,2,1,0:T(8,128)(2,1)} %param.5) | copy-start | bytes 4718596
  3.4 0.7 copy-start.3
  23.2 0.7 %copy-start.5 = (bf16[4,2,96,256]{3,2,1,0:T(8,128)(2,1)}, bf16[4,2,96,256]{3,2,1,0:T(8,128)(2,1)S(1)}, u32[]{:S(2)}) copy-start(bf16[4,2,96,256]{3,2,1,0:T(8,128)(2,1)S(1)} %get-tuple-element.9.halo_f) | copy-start | bytes 1179652
  24.0 0.7 %copy-start.7 = (bf16[4,2,96,256]{3,2,1,0:T(8,128)(2,1)}, bf16[4,2,96,256]{3,2,1,0:T(8,128)(2,1)S(1)}, u32[]{:S(2)}) copy-start(bf16[4,2,96,256]{3,2,1,0:T(8,128)(2,1)S(1)} %get-tuple-element.10.halo_g) | copy-start | bytes 1179652
  26.9 1.0 %copy-start.2 = (bf16[96,2592]{1,0:T(8,128)(2,1)S(1)}, bf16[96,2592]{1,0:T(8,128)(2,1)}, u32[]{:S(2)}) copy-start(bf16[96,2592]{1,0:T(8,128)(2,1)} %weight_ref.1) | copy-start | bytes 1492996
  26.9 1.0 %copy-start.4 = (s32[1,1,2]{2,1,0:T(1,128)S(1)}, s32[1,1,2]{2,1,0:T(1,128)}, u32[]{:S(2)}) copy-start(s32[1,1,2]{2,1,0:T(1,128)} %param.7) | copy-start | bytes 28
  26.9 1.1 %copy-start.6 = (bf16[4,2,96,256]{3,2,1,0:T(8,128)(2,1)S(1)}, bf16[4,2,96,256]{3,2,1,0:T(8,128)(2,1)}, u32[]{:S(2)}) copy-start(bf16[4,2,96,256]{3,2,1,0:T(8,128)(2,1)} %copy-done.5) | copy-start | bytes 1179652
  26.9 1.3 %copy-start.8 = (bf16[4,2,96,256]{3,2,1,0:T(8,128)(2,1)S(1)}, bf16[4,2,96,256]{3,2,1,0:T(8,128)(2,1)}, u32[]{:S(2)}) copy-start(bf16[4,2,96,256]{3,2,1,0:T(8,128)(2,1)} %copy-done.7) | copy-start | bytes 1179652
